TPU v7x, 256 devices: a whole 4x4x8 slice. The times are simulated.
256 devices in a mesh: seq: 64 (over z, y, core), grp: 4 (over x).
Axes of the slice: x: 4, y: 4, z: 8, core: 2. Of those that a mesh axis runs over, the one named last changes fastest.
Arguments:
- queries: bfloat16 [65536, 1024], P(('seq', 'grp')), may hold values from -5 to 5
- key_rows: bfloat16 [65536, 128], P(('seq', 'grp')), may hold values from -5 to 5
- value_rows: bfloat16 [65536, 128], P(('seq', 'grp')), may hold values from -6 to 6
- out_grad: bfloat16 [65536, 1024], P(('seq', 'grp')), may hold values from -6 to 6
- segment: int32 [65536], P(('seq', 'grp')), may hold values from 0 to 84, never falling along the last dimension, each value on 1 to 1536 neighbouring positions
Outputs:
- attended: bfloat16 [65536, 1024], P(('seq', 'grp'))
- query_grad: bfloat16 [65536, 1024], P(('seq', 'grp'))
- key_grad: float32 [65536, 128], P(('seq', 'grp'))
- value_grad: float32 [65536, 128], P(('seq', 'grp'))
Inputs may be any that keep to these rules, and one draw needn't show every extreme that they name: `segment`: segment numbers start at 0 and never fall along the sequence; every document holds 1 to 1536 tokens, and one holds exactly 1536.
All inputs are finite; a program needn't handle non-finite values.
Results may differ from a plain program's by a relative error of at most 0.019.
Values may be sent and summed in bfloat16 or wider, within the bound.
No kernel may reach another device: no remote copies, remote signals or barrier semaphores. Data moves between devices by JAX's collectives and lax.ppermute only.
A program may use at most 64 MiB of HBM per device.

v0:
```python
import jax
import jax.numpy as jnp
from jax import lax
from jax.sharding import PartitionSpec as P

SPAN = 6


def sent_together(arrays, axis, dim, along):
    ends, at = ([], 0)
    for a in arrays[:-1]:
        at += a.shape[along]
        ends.append(at)
    both = jnp.concatenate(arrays, axis=along)
    return tuple(jnp.split(lax.all_gather(both, axis, axis=dim, tiled=True), ends, axis=along))


def shifted(value, axis, steps):
    count = lax.axis_size(axis)
    first, last = (max(0, -steps), min(count, count - steps))
    return lax.ppermute(value, axis, [(source, source + steps) for source in range(first, last)])


def split_up(shard, dim, devices):
    before, after = (shard.shape[:dim], shard.shape[dim + 1 :])
    return jnp.moveaxis(shard.reshape(*before, devices, -1, *after), dim, 0)


def sent_and_summed(shard, axis, dim):
    devices = lax.axis_size(axis)
    tiles = lax.all_to_all(split_up(shard, dim, devices), axis, 0, 0, tiled=True)
    return jnp.sum(tiles.astype(jnp.float32), axis=0)


def on_device(queries, key_rows, value_rows, out_grad, segment):
    tokens = queries.shape[0]
    head_width = key_rows.shape[1]
    head_count = queries.shape[1] // head_width
    score_scale = head_width ** (-0.5)
    groups = lax.axis_size("grp")
    own_start = (lax.axis_index("seq") * groups + lax.axis_index("grp")) * tokens
    query_pos = own_start + jnp.arange(tokens, dtype=jnp.int32)
    query_heads = queries.reshape(tokens, head_count, head_width)
    grad_heads = out_grad.reshape(tokens, head_count, head_width)
    key_block = (
        *sent_together((key_rows, value_rows), "grp", 0, 1),
        lax.all_gather(segment, "grp", axis=0, tiled=True),
    )
    block_start = lax.axis_index("seq") * groups * tokens
    entries = [(key_block[0], key_block[1], key_block[2], block_start)]
    block_reach = -(-SPAN // groups)
    for distance in range(1, block_reach + 1):
        arrived = shifted((key_block[0], key_block[1], key_block[2]), "seq", distance)
        entries.append(
            (arrived[0], arrived[1], arrived[2], block_start - distance * groups * tokens)
        )

    def visible_of(entry_seg, entry_start):
        key_pos = entry_start + jnp.arange(entry_seg.shape[0], dtype=jnp.int32)
        allowed = (
            (entry_seg[None, :] == segment[:, None])
            & (key_pos[None, :] <= query_pos[:, None])
            & (key_pos[None, :] >= 0)
        )
        return allowed[:, None, :]

    def scores_of(entry_keys):
        return (
            jnp.einsum("thd,kd->thk", query_heads, entry_keys, preferred_element_type=jnp.float32)
            * score_scale
        )

    masks = [visible_of(entry[2], entry[3]) for entry in entries]
    running = (
        jnp.full((tokens, head_count), -1e30, jnp.float32),
        jnp.zeros((tokens, head_count), jnp.float32),
    )
    for entry, visible in zip(entries, masks):

        def first_pass(state_pair, entry=entry, visible=visible):
            row_max, row_sum = state_pair
            scores = scores_of(entry[0])
            new_max = jnp.maximum(row_max, jnp.max(jnp.where(visible, scores, -1e30), axis=-1))
            added = jnp.sum(jnp.where(visible, jnp.exp(scores - new_max[..., None]), 0.0), axis=-1)
            return (new_max, row_sum * jnp.exp(row_max - new_max) + added)

        running = first_pass(running)
    log_total = running[0] + jnp.log(running[1])
    output_sum = jnp.zeros((tokens, head_count, head_width), jnp.float32)
    for entry, visible in zip(entries, masks):

        def second_pass(partial_value, entry=entry, visible=visible):
            prob = jnp.where(visible, jnp.exp(scores_of(entry[0]) - log_total[..., None]), 0.0)
            weight = prob.astype(jnp.bfloat16)
            return partial_value + jnp.einsum(
                "thk,kd->thd", weight, entry[1], preferred_element_type=jnp.float32
            )

        output_sum = second_pass(output_sum)
    attended = output_sum.astype(jnp.bfloat16)
    row_dot = jnp.sum(grad_heads.astype(jnp.float32) * attended.astype(jnp.float32), axis=-1)
    query_total = jnp.zeros((tokens, head_count, head_width), jnp.float32)
    key_parts = []
    value_parts = []
    for entry, visible in zip(entries, masks):
        empty_rows = jnp.zeros((entry[0].shape[0], head_width), jnp.float32)

        def third_pass(triple, entry=entry, visible=visible):
            prob = jnp.where(visible, jnp.exp(scores_of(entry[0]) - log_total[..., None]), 0.0)
            weight = prob.astype(jnp.bfloat16)
            dprob = jnp.einsum(
                "thd,kd->thk", grad_heads, entry[1], preferred_element_type=jnp.float32
            )
            dscore = (score_scale * prob * (dprob - row_dot[..., None])).astype(jnp.bfloat16)
            query_next = triple[0] + jnp.einsum(
                "thk,kd->thd", dscore, entry[0], preferred_element_type=jnp.float32
            )
            key_part = jnp.einsum(
                "thk,thd->kd", dscore, query_heads, preferred_element_type=jnp.float32
            )
            value_part = jnp.einsum(
                "thk,thd->kd", weight, grad_heads, preferred_element_type=jnp.float32
            )
            return (query_next, key_part, value_part)

        query_total, key_part, value_part = third_pass((query_total, empty_rows, empty_rows))
        key_parts.append(key_part)
        value_parts.append(value_part)
    key_block_grad = key_parts[0]
    value_block_grad = value_parts[0]
    for distance in range(1, len(entries)):
        returned = (
            shifted(key_parts[distance].astype(jnp.bfloat16), "seq", -distance).astype(jnp.float32),
            shifted(value_parts[distance].astype(jnp.bfloat16), "seq", -distance).astype(
                jnp.float32
            ),
        )
        key_block_grad = key_block_grad + returned[0]
        value_block_grad = value_block_grad + returned[1]
    key_grad, value_grad = (
        sent_and_summed(key_block_grad.astype(jnp.bfloat16), "grp", 0),
        sent_and_summed(value_block_grad.astype(jnp.bfloat16), "grp", 0),
    )
    return (
        attended.reshape(tokens, head_count * head_width),
        query_total.astype(jnp.bfloat16).reshape(tokens, head_count * head_width),
        key_grad,
        value_grad,
    )


def solution(mesh):
    in_specs = (
        P(("seq", "grp"), None),
        P(("seq", "grp"), None),
        P(("seq", "grp"), None),
        P(("seq", "grp"), None),
        P(("seq", "grp")),
    )
    out_specs = (
        P(("seq", "grp"), None),
        P(("seq", "grp"), None),
        P(("seq", "grp"), None),
        P(("seq", "grp"), None),
    )
    return jax.shard_map(
        on_device, mesh=mesh, in_specs=in_specs, out_specs=out_specs, check_vma=False
    )
```

profile of v0, /device:TPU:120, one launch (start us, length us, event | category | flops | bytes accessed | tf_op | source)
XLA Modules:
  0.0 123.2 jit_solution(1365894006406280855)
XLA Ops:
  0.6 10.1 %all-gather = s32[4,1,256]{2,1,0:T(1,128)S(1)} all-gather(s32[1,1,256]{2,1,0:T(1,128)} %bitcast.217), channel_id=1, replica_groups=mesh['seq'=64,'grp'=4] {'grp'}, dimensions={0}, use_global_device_ids=true | all-gather | bytes 5120 | tf_op jit(solution)/shard_map/all_gather | solution.py:47
  10.7 4.7 %collective-permute-start.2 = (s32[1024]{0:T(1024)S(1)}, s32[1024]{0:T(1024)S(1)}, u32[]{:S(2)}, u32[]{:S(2)}) collective-permute-start(s32[1024]{0:T(1024)S(1)} %bitcast.214), channel_id=1, source_target_pairs={{0,8},{4,12},{8,16},{12,20},{16,24},{20,28},{24,32},{28,36},{32,40... | collective-permute-start | bytes 12296 | tf_op jit(solution)/shard_map/ppermute | solution.py:21
  18.3 13.4 %all_gather.7 = bf16[1024,256]{1,0:T(8,128)(2,1)S(1)} all-gather(bf16[256,256]{1,0:T(8,128)(2,1)S(1)} %pad_maximum_fusion), channel_id=1, replica_groups=mesh['seq'=64,'grp'=4] {'grp'}, dimensions={0}, use_global_device_ids=true | all-gather | bytes 655360 | tf_op jit(solution)/shard_map/all_gather | solution.py:15
  33.7 3.5 %collective-permute-start.5 = (bf16[1024,128]{1,0:T(8,128)(2,1)S(1)}, bf16[1024,128]{1,0:T(8,128)(2,1)}, u32[]{:S(2)}, u32[]{:S(2)}) collective-permute-start(bf16[1024,128]{1,0:T(8,128)(2,1)S(1)} %get-tuple-element.14), channel_id=1, source_target_pairs={{0,8},{4,12},{8,16},{12,20},{16,24},{20,28},{24,32},{28,36},{32,40... | collective-permute-start | bytes 786440 | tf_op jit(solution)/shard_map/ppermute | solution.py:21
  37.2 3.3 %collective-permute-start.1 = (bf16[1024,128]{1,0:T(8,128)(2,1)S(1)}, bf16[1024,128]{1,0:T(8,128)(2,1)S(1)}, u32[]{:S(2)}, u32[]{:S(2)}) collective-permute-start(bf16[1024,128]{1,0:T(8,128)(2,1)S(1)} %get-tuple-element.15), channel_id=1, source_target_pairs={{0,4},{4,8},{8,12},{12,16},{16,20},{20,24},{24,28},{28,32},{32,36}... | collective-permute-start | bytes 786440 | tf_op jit(solution)/shard_map/ppermute | solution.py:21
  41.8 3.1 %collective-permute-start.3 = (bf16[1024,128]{1,0:T(8,128)(2,1)S(1)}, bf16[1024,128]{1,0:T(8,128)(2,1)S(1)}, u32[]{:S(2)}, u32[]{:S(2)}) collective-permute-start(bf16[1024,128]{1,0:T(8,128)(2,1)S(1)} %get-tuple-element.15), channel_id=1, source_target_pairs={{0,8},{4,12},{8,16},{12,20},{16,24},{20,28},{24,32},{28,36},{32,40... | collective-permute-start | bytes 786440 | tf_op jit(solution)/shard_map/ppermute | solution.py:21
  44.9 2.3 %and_and_fusion.2 = (pred[256,1024]{0,1:T(8,128)(4,1)S(1)}, pred[256,1024]{0,1:T(8,128)(4,1)S(1)}, pred[256,1024]{0,1:T(8,128)(4,1)S(1)}) fusion(s32[256]{0:T(256)S(1)} %iota_add_fusion.3, s32[256]{0:T(256)} %param.9, s32[1024]{0:T(1024)S(1)} %iota_add_fusion.2, s32[1024]{0:T(1024)S(1)} %bitcast.216, pred[1024]{0:T(1024)(128)(4,1)S(1)} %broadcast_compare_fusion.2, ...), kind=kLoop, calls=%fused_computation.55 | loop fusion | flops 3145728 | bytes 816128 | tf_op jit(solution)/shard_map/and | solution.py:61
  50.1 2.8 %collective-permute-done.3 = bf16[1024,128]{1,0:T(8,128)(2,1)S(1)} collective-permute-done((bf16[1024,128]{1,0:T(8,128)(2,1)S(1)}, bf16[1024,128]{1,0:T(8,128)(2,1)S(1)}, u32[]{:S(2)}, u32[]{:S(2)}) %collective-permute-start.3) | collective-permute-done | bytes 262176 | tf_op jit(solution)/shard_map/ppermute | solution.py:21
  56.1 3.6 %fusion.6 = (f32[256,8]{0,1:T(8,128)S(1)}, f32[256,8]{0,1:T(8,128)S(1)}) fusion(f32[1024,256,8]{1,0,2:T(8,128)S(1)} %get-tuple-element.21, f32[256,8]{0,1:T(8,128)S(1)} %get-tuple-element.12, pred[256,1024]{0,1:T(8,128)(4,1)S(1)} %get-tuple-element.19, f32[256,8]{0,1:T(8,128)S(1)} %get-tuple-element.13, f32[1024,256,8]{1,0,2:T(8,128)S(1)} %get-tuple-element.23, ...), kind=kLoop, calls=%fused_computation.12 | loop fusion | flops 16773120 | bytes 17334272 | tf_op jit(solution)/shard_map/reduce_sum | solution.py:84
  66.3 2.0 %collective-permute-start.9 = (bf16[1024,128]{1,0:T(8,128)(2,1)S(1)}, bf16[1024,128]{1,0:T(8,128)(2,1)S(1)}, u32[]{:S(2)}, u32[]{:S(2)}) collective-permute-start(bf16[1024,128]{1,0:T(8,128)(2,1)S(1)} %fusion.29), channel_id=1, source_target_pairs={{8,0},{12,4},{16,8},{20,12},{24,16},{28,20},{32,24},{36,28},{40,32... | collective-permute-start | bytes 786440 | tf_op jit(solution)/shard_map/ppermute | solution.py:21
  70.3 2.1 %convolution_add_fusion.3 = f32[256,8,128]{0,2,1:T(8,128)S(1)} fusion(f32[256,8,128]{0,2,1:T(8,128)S(1)} %fusion.44, bf16[1024,128]{1,0:T(8,128)(2,1)S(1)} %collective-permute-done.4, f32[1024,256,8]{1,0,2:T(8,128)S(1)} %get-tuple-element.23, f32[256,8]{0,1:T(8,128)S(1)} %log_add_fusion, pred[256,1024]{0,1:T(8,128)(4,1)S(1)} %get-tuple-element.18), kind=kOutput, calls=%fused_computation.39 | convolution fusion | flops 545521664 | bytes 11018240 | tf_op jit(solution)/shard_map/thk,kd->thd/dot_general | solution.py:95
  72.4 2.7 %multiply_reduce_fusion = (f32[256,8]{0,1:T(8,128)S(1)}, bf16[256,8,128]{0,2,1:T(8,128)(2,1)S(1)}) fusion(bf16[256,1024]{0,1:T(8,128)(2,1)S(1)} %copy.45, f32[256,8,128]{0,2,1:T(8,128)S(1)} %convolution_add_fusion.3, bf16[1024,128]{1,0:T(8,128)(2,1)} %collective-permute-done.5, f32[1024,256,8]{1,0,2:T(8,128)S(1)} %get-tuple-element.21, ...), kind=kOutput, calls=%fused_computation.52 | convolution fusion | flops 546830336 | bytes 11026432 | tf_op jit(solution)/shard_map/thk,kd->thd/dot_general | solution.py:95
  75.1 4.4 %fusion.2 = bf16[256,8,1024]{0,2,1:T(8,128)(2,1)} fusion(f32[1024,256,8]{1,0,2:T(8,128)S(1)} %get-tuple-element.25, f32[256,8]{0,1:T(8,128)S(1)} %get-tuple-element.26, f32[256,8]{0,1:T(8,128)S(1)} %log_add_fusion, pred[256,1024]{0,1:T(8,128)(4,1)S(1)} %get-tuple-element.17, bf16[256,8,128]{0,2,1:T(8,128)(2,1)S(1)} %bitcast.210, ...), kind=kOutput, calls=%fused_computation.5 | convolution fusion | flops 551550976 | bytes 13647872 | tf_op jit(solution)/shard_map/thd,kd->thk/dot_general | solution.py:111
  79.5 4.0 %fusion = bf16[256,8,1024]{0,2,1:T(8,128)(2,1)S(1)} fusion(f32[1024,256,8]{1,0,2:T(8,128)S(1)} %get-tuple-element.21, f32[256,8]{0,1:T(8,128)S(1)} %get-tuple-element.26, f32[256,8]{0,1:T(8,128)S(1)} %log_add_fusion, pred[256,1024]{0,1:T(8,128)(4,1)S(1)} %get-tuple-element.19, bf16[256,8,128]{0,2,1:T(8,128)(2,1)S(1)} %bitcast.211, ...), kind=kOutput, calls=%fused_computation.1 | convolution fusion | flops 551550976 | bytes 13647872 | tf_op jit(solution)/shard_map/thd,kd->thk/dot_general | solution.py:111
  83.5 2.1 %fusion.27 = bf16[1024,128]{1,0:T(8,128)(2,1)} fusion(bf16[256,8,1024]{0,2,1:T(8,128)(2,1)S(1)} %fusion, bf16[256,1024]{1,0:T(8,128)(2,1)S(1)} %copy-done), kind=kOutput, calls=%fused_computation.49 | convolution fusion | flops 537001984 | bytes 4980736 | tf_op jit(solution)/shard_map/thk,thd->kd/dot_general | solution.py:118
  85.6 3.0 %fusion.1 = bf16[256,8,1024]{0,2,1:T(8,128)(2,1)S(1)} fusion(f32[1024,256,8]{1,0,2:T(8,128)S(1)} %get-tuple-element.23, f32[256,8]{0,1:T(8,128)S(1)} %get-tuple-element.26, f32[256,8]{0,1:T(8,128)S(1)} %log_add_fusion, pred[256,1024]{0,1:T(8,128)(4,1)S(1)} %get-tuple-element.18, bf16[256,8,128]{0,2,1:T(8,128)(2,1)S(1)} %bitcast.212, ...), kind=kOutput, calls=%fused_computation.3 | convolution fusion | flops 551550976 | bytes 13647872 | tf_op jit(solution)/shard_map/thd,kd->thk/dot_general | solution.py:111
  88.6 2.0 %fusion.26 = bf16[1024,128]{1,0:T(8,128)(2,1)} fusion(bf16[256,8,1024]{0,2,1:T(8,128)(2,1)S(1)} %fusion.1, bf16[256,1024]{1,0:T(8,128)(2,1)S(1)} %copy-done), kind=kOutput, calls=%fused_computation.48 | convolution fusion | flops 537001984 | bytes 4980736 | tf_op jit(solution)/shard_map/thk,thd->kd/dot_general | solution.py:118
  90.6 2.3 %collective-permute-start.6 = (bf16[1024,128]{1,0:T(8,128)(2,1)}, bf16[1024,128]{1,0:T(8,128)(2,1)}, u32[]{:S(2)}, u32[]{:S(2)}) collective-permute-start(bf16[1024,128]{1,0:T(8,128)(2,1)} %fusion.26), channel_id=1, source_target_pairs={{4,0},{8,4},{12,8},{16,12},{20,16},{24,20},{28,24},{32,28},{36,32}... | collective-permute-start | bytes 786440 | tf_op jit(solution)/shard_map/ppermute | solution.py:21
  92.9 3.6 %collective-permute-start.7 = (bf16[1024,128]{1,0:T(8,128)(2,1)}, bf16[1024,128]{1,0:T(8,128)(2,1)}, u32[]{:S(2)}, u32[]{:S(2)}) collective-permute-start(bf16[1024,128]{1,0:T(8,128)(2,1)} %fusion.27), channel_id=1, source_target_pairs={{8,0},{12,4},{16,8},{20,12},{24,16},{28,20},{32,24},{36,28},{40,32... | collective-permute-start | bytes 786440 | tf_op jit(solution)/shard_map/ppermute | solution.py:21
  98.9 3.4 %all-to-all-start.1 = ((bf16[4,256,128]{2,1,0:T(8,128)(2,1)}), bf16[4,256,128]{2,1,0:T(8,128)(2,1)S(1)}, u32[]{:S(2)}, u32[]{:S(2)}) async-start(bf16[4,256,128]{2,1,0:T(8,128)(2,1)} %bitcast.30), calls=%async_computation.1 | async-start | bytes 524288 | tf_op jit(solution)/shard_map/all_to_all | solution.py:31
  102.3 5.9 %collective-permute-done.7 = bf16[1024,128]{1,0:T(8,128)(2,1)} collective-permute-done((bf16[1024,128]{1,0:T(8,128)(2,1)}, bf16[1024,128]{1,0:T(8,128)(2,1)}, u32[]{:S(2)}, u32[]{:S(2)}) %collective-permute-start.7) | collective-permute-done | bytes 262176 | tf_op jit(solution)/shard_map/ppermute | solution.py:21
  108.2 4.3 %add_convert_fusion.1 = bf16[1024,128]{1,0:T(8,128)(2,1)} fusion(bf16[1024,128]{1,0:T(8,128)(2,1)} %collective-permute-done.7, bf16[1024,128]{1,0:T(8,128)(2,1)} %collective-permute-done.6, bf16[256,8,1024]{0,2,1:T(8,128)(2,1)} %fusion.2, bf16[256,1024]{1,0:T(8,128)(2,1)S(1)} %copy-done), kind=kOutput, calls=%fused_computation.68 | convolution fusion | flops 537526272 | bytes 5505024 | tf_op jit(solution)/shard_map/thk,thd->kd/dot_general | solution.py:118
  112.4 3.4 %all-to-all-start = ((bf16[4,256,128]{2,1,0:T(8,128)(2,1)}), bf16[4,256,128]{2,1,0:T(8,128)(2,1)S(1)}, u32[]{:S(2)}, u32[]{:S(2)}) async-start(bf16[4,256,128]{2,1,0:T(8,128)(2,1)} %bitcast.26), calls=%async_computation | async-start | bytes 524288 | tf_op jit(solution)/shard_map/all_to_all | solution.py:31
  115.9 3.0 %fusion.25 = bf16[256,8,128]{0,2,1:T(8,128)(2,1)S(1)} fusion(f32[256,8,128]{0,2,1:T(8,128)S(1)} %convolution_add_fusion.1, bf16[256,8,1024]{0,2,1:T(8,128)(2,1)} %copy-done.1, bf16[1024,128]{1,0:T(8,128)(2,1)S(1)} %collective-permute-done.3), kind=kOutput, calls=%fused_computation.41 | convolution fusion | flops 537395200 | bytes 6029312 | tf_op jit(solution)/shard_map/thk,kd->thd/dot_general | solution.py:115
  (50 shorter events, 27.2 us)
Async XLA Ops:
  0.6 46.6 %copy-start = (bf16[256,1024]{1,0:T(8,128)(2,1)S(1)}, bf16[256,1024]{1,0:T(8,128)(2,1)}, u32[]{:S(2)}) copy-start(bf16[256,1024]{1,0:T(8,128)(2,1)} %param.5) | copy-start | bytes 1572868
  10.7 31.1 %collective-permute-start.2 = (s32[1024]{0:T(1024)S(1)}, s32[1024]{0:T(1024)S(1)}, u32[]{:S(2)}, u32[]{:S(2)}) collective-permute-start(s32[1024]{0:T(1024)S(1)} %bitcast.214), channel_id=1, source_target_pairs={{0,8},{4,12},{8,16},{12,20},{16,24},{20,28},{24,32},{28,36},{32,40... | collective-permute-start | bytes 12296 | tf_op jit(solution)/shard_map/ppermute | solution.py:21
  15.4 29.5 %collective-permute-start = (s32[1024]{0:T(1024)S(1)}, s32[1024]{0:T(1024)S(1)}, u32[]{:S(2)}, u32[]{:S(2)}) collective-permute-start(s32[1024]{0:T(1024)S(1)} %bitcast.215), channel_id=1, source_target_pairs={{0,4},{4,8},{8,12},{12,16},{16,20},{20,24},{24,28},{28,32},{32,36}... | collective-permute-start | bytes 12296 | tf_op jit(solution)/shard_map/ppermute | solution.py:21
  31.7 38.5 %collective-permute-start.4 = (bf16[1024,128]{1,0:T(8,128)(2,1)S(1)}, bf16[1024,128]{1,0:T(8,128)(2,1)S(1)}, u32[]{:S(2)}, u32[]{:S(2)}) collective-permute-start(bf16[1024,128]{1,0:T(8,128)(2,1)S(1)} %get-tuple-element.14), channel_id=1, source_target_pairs={{0,4},{4,8},{8,12},{12,16},{16,20},{20,24},{24,28},{28,32},{32,36}... | collective-permute-start | bytes 786440 | tf_op jit(solution)/shard_map/ppermute | solution.py:21
  33.7 38.7 %collective-permute-start.5 = (bf16[1024,128]{1,0:T(8,128)(2,1)S(1)}, bf16[1024,128]{1,0:T(8,128)(2,1)}, u32[]{:S(2)}, u32[]{:S(2)}) collective-permute-start(bf16[1024,128]{1,0:T(8,128)(2,1)S(1)} %get-tuple-element.14), channel_id=1, source_target_pairs={{0,8},{4,12},{8,16},{12,20},{16,24},{20,28},{24,32},{28,36},{32,40... | collective-permute-start | bytes 786440 | tf_op jit(solution)/shard_map/ppermute | solution.py:21
  37.2 11.5 %collective-permute-start.1 = (bf16[1024,128]{1,0:T(8,128)(2,1)S(1)}, bf16[1024,128]{1,0:T(8,128)(2,1)S(1)}, u32[]{:S(2)}, u32[]{:S(2)}) collective-permute-start(bf16[1024,128]{1,0:T(8,128)(2,1)S(1)} %get-tuple-element.15), channel_id=1, source_target_pairs={{0,4},{4,8},{8,12},{12,16},{16,20},{20,24},{24,28},{28,32},{32,36}... | collective-permute-start | bytes 786440 | tf_op jit(solution)/shard_map/ppermute | solution.py:21
  41.8 11.1 %collective-permute-start.3 = (bf16[1024,128]{1,0:T(8,128)(2,1)S(1)}, bf16[1024,128]{1,0:T(8,128)(2,1)S(1)}, u32[]{:S(2)}, u32[]{:S(2)}) collective-permute-start(bf16[1024,128]{1,0:T(8,128)(2,1)S(1)} %get-tuple-element.15), channel_id=1, source_target_pairs={{0,8},{4,12},{8,16},{12,20},{16,24},{20,28},{24,32},{28,36},{32,40... | collective-permute-start | bytes 786440 | tf_op jit(solution)/shard_map/ppermute | solution.py:21
  66.3 31.8 %collective-permute-start.9 = (bf16[1024,128]{1,0:T(8,128)(2,1)S(1)}, bf16[1024,128]{1,0:T(8,128)(2,1)S(1)}, u32[]{:S(2)}, u32[]{:S(2)}) collective-permute-start(bf16[1024,128]{1,0:T(8,128)(2,1)S(1)} %fusion.29), channel_id=1, source_target_pairs={{8,0},{12,4},{16,8},{20,12},{24,16},{28,20},{32,24},{36,28},{40,32... | collective-permute-start | bytes 786440 | tf_op jit(solution)/shard_map/ppermute | solution.py:21
  68.3 29.7 %collective-permute-start.8 = (bf16[1024,128]{1,0:T(8,128)(2,1)S(1)}, bf16[1024,128]{1,0:T(8,128)(2,1)S(1)}, u32[]{:S(2)}, u32[]{:S(2)}) collective-permute-start(bf16[1024,128]{1,0:T(8,128)(2,1)S(1)} %fusion.28), channel_id=1, source_target_pairs={{4,0},{8,4},{12,8},{16,12},{20,16},{24,20},{28,24},{32,28},{36,32}... | collective-permute-start | bytes 786440 | tf_op jit(solution)/shard_map/ppermute | solution.py:21
  70.2 2.1 %copy-start.3 = (bf16[1024,128]{1,0:T(8,128)(2,1)}, bf16[1024,128]{1,0:T(8,128)(2,1)S(1)}, u32[]{:S(2)}) copy-start(bf16[1024,128]{1,0:T(8,128)(2,1)S(1)} %collective-permute-done.4) | copy-start | bytes 786436
  79.5 6.1 %copy-start.4 = (bf16[1024,128]{1,0:T(8,128)(2,1)S(1)}, bf16[1024,128]{1,0:T(8,128)(2,1)}, u32[]{:S(2)}) copy-start(bf16[1024,128]{1,0:T(8,128)(2,1)} %copy-done.3) | copy-start | bytes 786436
  83.5 5.1 %copy-start.1 = (bf16[256,8,1024]{0,2,1:T(8,128)(2,1)}, bf16[256,8,1024]{0,2,1:T(8,128)(2,1)S(1)}, u32[]{:S(2)}) copy-start(bf16[256,8,1024]{0,2,1:T(8,128)(2,1)S(1)} %fusion) | copy-start | bytes 12582916
  85.6 10.9 %copy-start.2 = (bf16[256,8,1024]{0,2,1:T(8,128)(2,1)S(1)}, bf16[256,8,1024]{0,2,1:T(8,128)(2,1)}, u32[]{:S(2)}) copy-start(bf16[256,8,1024]{0,2,1:T(8,128)(2,1)} %fusion.2) | copy-start | bytes 12582916
  90.6 11.7 %collective-permute-start.6 = (bf16[1024,128]{1,0:T(8,128)(2,1)}, bf16[1024,128]{1,0:T(8,128)(2,1)}, u32[]{:S(2)}, u32[]{:S(2)}) collective-permute-start(bf16[1024,128]{1,0:T(8,128)(2,1)} %fusion.26), channel_id=1, source_target_pairs={{4,0},{8,4},{12,8},{16,12},{20,16},{24,20},{28,24},{32,28},{36,32}... | collective-permute-start | bytes 786440 | tf_op jit(solution)/shard_map/ppermute | solution.py:21
  92.9 15.3 %collective-permute-start.7 = (bf16[1024,128]{1,0:T(8,128)(2,1)}, bf16[1024,128]{1,0:T(8,128)(2,1)}, u32[]{:S(2)}, u32[]{:S(2)}) collective-permute-start(bf16[1024,128]{1,0:T(8,128)(2,1)} %fusion.27), channel_id=1, source_target_pairs={{8,0},{12,4},{16,8},{20,12},{24,16},{28,20},{32,24},{36,28},{40,32... | collective-permute-start | bytes 786440 | tf_op jit(solution)/shard_map/ppermute | solution.py:21
  98.9 13.6 %all-to-all-start.1 = ((bf16[4,256,128]{2,1,0:T(8,128)(2,1)}), bf16[4,256,128]{2,1,0:T(8,128)(2,1)S(1)}, u32[]{:S(2)}, u32[]{:S(2)}) async-start(bf16[4,256,128]{2,1,0:T(8,128)(2,1)} %bitcast.30), calls=%async_computation.1 | async-start | bytes 524288 | tf_op jit(solution)/shard_map/all_to_all | solution.py:31
  112.4 10.1 %all-to-all-start = ((bf16[4,256,128]{2,1,0:T(8,128)(2,1)}), bf16[4,256,128]{2,1,0:T(8,128)(2,1)S(1)}, u32[]{:S(2)}, u32[]{:S(2)}) async-start(bf16[4,256,128]{2,1,0:T(8,128)(2,1)} %bitcast.26), calls=%async_computation | async-start | bytes 524288 | tf_op jit(solution)/shard_map/all_to_all | solution.py:31
where the time goes:
time: 124 us; the launch traced here: 123 us
  matrix products  39.7 us (32%)
  starting transfers between devices  35 us (28%)
  blocking collectives  23.5 us (19%)
  other arithmetic  10.8 us (9%)
  waiting for transfers between devices  9.73 us (8%)
  local copies, waits for them, and re-layouts  3.31 us (3%)
    ppermute x10, starting transfers between devices, shifted(): lax.ppermute(value, axis, [(source, source + steps) for source in range(f...  28.2 us
    all_gather x1, blocking collectives, sent_together(): lax.all_gather(both, axis, axis=dim, tiled=True)  13.4 us
    dot_general x3, matrix products, third_pass(): jnp.einsum('thd,kd->thk', grad_heads, entry[1], preferred_element_type=jn...  11.4 us
    all_gather x1, blocking collectives, on_device(): lax.all_gather(segment, 'grp', axis=0, tiled=True)  10.1 us
    ppermute x10, waiting for transfers between devices, shifted(): lax.ppermute(value, axis, [(source, source + steps) for source in range(f...  8.73 us
    dot_general x3, matrix products, third_pass(): jnp.einsum('thk,thd->kd', dscore, query_heads, preferred_element_type=jnp...  8.31 us
    all_to_all x2, starting transfers between devices, sent_and_summed(): lax.all_to_all(split_up(shard, dim, devices), axis, 0, 0, tiled=True)  6.81 us
    dot_general x3, matrix products, second_pass(): jnp.einsum('thk,kd->thd', weight, entry[1], preferred_element_type=jnp.fl...  6.52 us
  transfers between devices with their start and end apart: 12, of which 3 were waited for; matrix products, arithmetic and copies ran while one was open for 43% of the time, Pallas kernels for 0%

commit v1 on v0

v1 whole, which is shorter than its diff:
```python
import functools
import math

import jax
import jax.numpy as jnp
from jax import lax
from jax.experimental import pallas as pl
from jax.experimental.pallas import tpu as pltpu
from jax.sharding import PartitionSpec as P

AXES = ("seq", "grp")
BACK = 6
HIDE = -1e30


def wrapped(value, steps):
    count = lax.axis_size(AXES)
    return lax.ppermute(value, AXES, [(i, (i + steps) % count) for i in range(count)])


def nt(a, b):
    return lax.dot_general(a, b, (((1,), (1,)), ((), ())), preferred_element_type=jnp.float32)


def nn(a, b):
    return lax.dot_general(a, b, (((1,), (0,)), ((), ())), preferred_element_type=jnp.float32)


def attention_kernel(
    heads,
    q_ref,
    g_ref,
    *refs,
):
    blocks = refs[: BACK + 1]
    o_ref, dq_ref, own_ref = refs[BACK + 1 : BACK + 4]
    parts = refs[BACK + 4 : 2 * BACK + 4]
    kt, vt, qs, gs, sc, ex, bias, dots = refs[2 * BACK + 4 :]
    tokens = q_ref.shape[0]
    width = q_ref.shape[1] // heads
    scale = width**-0.5
    scale2 = scale * math.log2(math.e)
    chunks = BACK + 1

    def rows(c):
        return slice(c * tokens, (c + 1) * tokens)

    own_seg = blocks[0][tokens : tokens + 8, :].astype(jnp.float32)
    row_seg = own_seg[0:1, :]
    key_seg = jnp.transpose(own_seg)[:, 0:1]
    key_at = lax.broadcasted_iota(jnp.int32, (tokens, tokens), 0)
    row_at = lax.broadcasted_iota(jnp.int32, (tokens, tokens), 1)
    bias[rows(0), :] = jnp.where((key_seg == row_seg) & (key_at <= row_at), 0.0, HIDE)
    first = row_seg[:, 0:1]
    for c in range(1, chunks):
        seg = blocks[c][tokens : tokens + 8, :].astype(jnp.float32)[0:1, :]
        count = jnp.sum(jnp.where(seg == first, 1.0, 0.0), axis=1, keepdims=True)
        shown = (key_at.astype(jnp.float32) >= tokens - count) & (row_seg == first)
        bias[rows(c), :] = jnp.where(shown, 0.0, HIDE)
    for c in range(chunks):
        kt[:, rows(c)] = jnp.transpose(blocks[c][0:tokens, 0:width])
        vt[:, rows(c)] = jnp.transpose(blocks[c][0:tokens, width : 2 * width])

    def forward(h, carry):
        lanes = pl.ds(pl.multiple_of(h * width, width), width)
        at = pl.ds(pl.multiple_of(h * tokens, tokens), tokens)
        q = q_ref[:, lanes]
        qs[at, :] = q
        top = jnp.full((1, tokens), HIDE, jnp.float32)
        for c in range(chunks):
            s = nt(blocks[c][0:tokens, 0:width], q) * scale2 + bias[rows(c), :]
            sc[rows(c), :] = s
            top = jnp.maximum(top, jnp.max(s, axis=0, keepdims=True))
        total = jnp.zeros((1, tokens), jnp.float32)
        for c in range(chunks):
            e = jnp.exp2(sc[rows(c), :] - top)
            total = total + jnp.sum(e, axis=0, keepdims=True)
            ex[rows(c), at] = e.astype(jnp.bfloat16)
        inv = 1.0 / total
        out = jnp.transpose(nn(vt[...], ex[:, at]) * inv)
        o_ref[:, lanes] = out.astype(o_ref.dtype)
        inv_rows = jnp.transpose(jnp.broadcast_to(inv, (8, tokens)))[:, 0:1]
        g = (g_ref[:, lanes].astype(jnp.float32) * inv_rows).astype(jnp.bfloat16)
        gs[at, :] = g
        prod = g.astype(jnp.float32) * out
        high = prod.astype(jnp.bfloat16)
        low = (prod - high.astype(jnp.float32)).astype(jnp.bfloat16)
        ones = jnp.ones((8, width), jnp.bfloat16)
        dots[:, at] = nt(ones, high) + nt(ones, low)
        return carry

    lax.fori_loop(0, heads, forward, 0)

    for c in range(chunks):
        part = own_ref if c == 0 else parts[c - 1]
        part[:, width : 2 * width] = nn(ex[rows(c), :], gs[...]).astype(part.dtype)

        def backward(h, carry, c=c):
            at = pl.ds(pl.multiple_of(h * tokens, tokens), tokens)
            d = nt(blocks[c][0:tokens, width : 2 * width], gs[at, :]) - dots[0:1, at]
            ex[rows(c), at] = (ex[rows(c), at].astype(jnp.float32) * d).astype(jnp.bfloat16)
            return carry

        lax.fori_loop(0, heads, backward, 0)
        part[:, 0:width] = (nn(ex[rows(c), :], qs[...]) * scale).astype(part.dtype)

    def query_step(h, carry):
        lanes = pl.ds(pl.multiple_of(h * width, width), width)
        at = pl.ds(pl.multiple_of(h * tokens, tokens), tokens)
        dq_t = nn(kt[...], ex[:, at]) * scale
        dq_ref[:, lanes] = jnp.transpose(dq_t).astype(dq_ref.dtype)
        return carry

    lax.fori_loop(0, heads, query_step, 0)


def attention(queries, out_grad, blocks):
    tokens = queries.shape[0]
    width = blocks[0].shape[1] // 2
    heads = queries.shape[1] // width
    keys = (BACK + 1) * tokens
    vmem = pl.BlockSpec(memory_space=pltpu.VMEM)
    return pl.pallas_call(
        functools.partial(attention_kernel, heads),
        out_shape=(
            jax.ShapeDtypeStruct(queries.shape, jnp.bfloat16),
            jax.ShapeDtypeStruct(queries.shape, jnp.bfloat16),
            jax.ShapeDtypeStruct((tokens, 2 * width), jnp.float32),
        )
        + (jax.ShapeDtypeStruct((tokens, 2 * width), jnp.bfloat16),) * BACK,
        in_specs=[vmem] * (BACK + 3),
        out_specs=(vmem,) * (BACK + 3),
        scratch_shapes=[
            pltpu.VMEM((width, keys), jnp.bfloat16),
            pltpu.VMEM((width, keys), jnp.bfloat16),
            pltpu.VMEM((heads * tokens, width), jnp.bfloat16),
            pltpu.VMEM((heads * tokens, width), jnp.bfloat16),
            pltpu.VMEM((keys, tokens), jnp.float32),
            pltpu.VMEM((keys, heads * tokens), jnp.bfloat16),
            pltpu.VMEM((keys, tokens), jnp.float32),
            pltpu.VMEM((8, heads * tokens), jnp.float32),
        ],
        compiler_params=pltpu.CompilerParams(vmem_limit_bytes=40 * 1024 * 1024),
        name="attention",
    )(queries, out_grad, *blocks)


def on_device(queries, key_rows, value_rows, out_grad, segment):
    tokens, width = key_rows.shape
    marks = jnp.broadcast_to(segment.astype(jnp.bfloat16)[None, :], (16, tokens))
    own = jnp.concatenate([jnp.concatenate([key_rows, value_rows], axis=1), marks], axis=0)
    blocks = [own] + [wrapped(own, d) for d in range(1, BACK + 1)]
    attended, query_grad, total, *parts = attention(queries, out_grad, blocks)
    for d in range(1, BACK + 1):
        total = total + wrapped(parts[d - 1], -d).astype(jnp.float32)
    return attended, query_grad, total[:, :width], total[:, width:]


def solution(mesh):
    spec = P(AXES, None)
    return jax.shard_map(
        on_device,
        mesh=mesh,
        in_specs=(spec, spec, spec, spec, P(AXES)),
        out_specs=(spec,) * 4,
        check_vma=False,
    )
```

time: 124 us -> 79.5 us (0.64)
  the two profiles are of different devices: /device:TPU:120 before, /device:TPU:0 now
where the time goes in v1:
time: 79.5 us; the launch traced here: 78.2 us
  Pallas kernels  32.3 us (41%)
  waiting for transfers between devices  31.4 us (39%)
  starting transfers between devices  9.28 us (12%)
  local copies, waits for them, and re-layouts  2.81 us (4%)
  other arithmetic  1.7 us (2%)
    pallas_call x1, Pallas kernels, attention(): pl.pallas_call(functools.partial(attention_kernel, heads), out_shape=(jax...  32.3 us
    ppermute x12, waiting for transfers between devices, wrapped(): lax.ppermute(value, AXES, [(i, (i + steps) % count) for i in range(count)])  31.4 us
    ppermute x12, starting transfers between devices, wrapped(): lax.ppermute(value, AXES, [(i, (i + steps) % count) for i in range(count)])  9.28 us
    unnamed x4, local copies, waits for them, and re-layouts  2.08 us
  transfers between devices with their start and end apart: 12, of which 9 were waited for; matrix products, arithmetic and copies ran while one was open for 0% of the time, Pallas kernels for 0%

profile of v1, /device:TPU:0, one launch (start us, length us, event | category | flops | bytes accessed | tf_op | source)
XLA Modules:
  0.0 78.2 jit_solution(16098276452596936107)
XLA Ops:
  0.6 0.7 convert_element_type.21
  1.3 0.9 %pad_maximum_fusion.refs_0_ = bf16[272,256]{1,0:T(8,128)(2,1)S(1)} fusion(bf16[16,256]{1,0:T(8,128)(2,1)S(1)} %broadcast_in_dim.2, bf16[256,128]{1,0:T(8,128)(2,1)} %param.7, bf16[256,128]{1,0:T(8,128)(2,1)} %param.6), kind=kLoop, calls=%fused_computation.1 | loop fusion | flops 417792 | bytes 278528 | tf_op jit(solution)/shard_map/concatenate | solution.py:151
  2.2 0.8 %collective-permute-start.5 = (bf16[272,256]{1,0:T(8,128)(2,1)S(1)}, bf16[272,256]{1,0:T(8,128)(2,1)S(1)}, u32[]{:S(2)}, u32[]{:S(2)}) collective-permute-start(bf16[272,256]{1,0:T(8,128)(2,1)S(1)} %pad_maximum_fusion.refs_0_), channel_id=1, source_target_pairs={{0,6},{1,7},{2,8},{3,9},{4,10},{5,11},{6,12},{7,13},{8,14},{9,15},... | collective-permute-start | bytes 417800 | tf_op jit(solution)/shard_map/ppermute | solution.py:18
  3.0 1.9 %collective-permute-start.4 = (bf16[272,256]{1,0:T(8,128)(2,1)S(1)}, bf16[272,256]{1,0:T(8,128)(2,1)S(1)}, u32[]{:S(2)}, u32[]{:S(2)}) collective-permute-start(bf16[272,256]{1,0:T(8,128)(2,1)S(1)} %pad_maximum_fusion.refs_0_), channel_id=1, source_target_pairs={{0,5},{1,6},{2,7},{3,8},{4,9},{5,10},{6,11},{7,12},{8,13},{9,14},{... | collective-permute-start | bytes 417800 | tf_op jit(solution)/shard_map/ppermute | solution.py:18
  4.9 3.8 %collective-permute-start.2 = (bf16[272,256]{1,0:T(8,128)(2,1)S(1)}, bf16[272,256]{1,0:T(8,128)(2,1)S(1)}, u32[]{:S(2)}, u32[]{:S(2)}) collective-permute-start(bf16[272,256]{1,0:T(8,128)(2,1)S(1)} %pad_maximum_fusion.refs_0_), channel_id=1, source_target_pairs={{0,3},{1,4},{2,5},{3,6},{4,7},{5,8},{6,9},{7,10},{8,11},{9,12},{10... | collective-permute-start | bytes 417800 | tf_op jit(solution)/shard_map/ppermute | solution.py:18
  8.7 0.0 collective-permute-start.1
  8.7 9.9 %collective-permute-done.5.refs_6_ = bf16[272,256]{1,0:T(8,128)(2,1)S(1)} collective-permute-done((bf16[272,256]{1,0:T(8,128)(2,1)S(1)}, bf16[272,256]{1,0:T(8,128)(2,1)S(1)}, u32[]{:S(2)}, u32[]{:S(2)}) %collective-permute-start.5) | collective-permute-done | bytes 139296 | tf_op jit(solution)/shard_map/ppermute | solution.py:18
  18.5 0.0 collective-permute-start
  18.6 2.4 %collective-permute-done.4.refs_5_ = bf16[272,256]{1,0:T(8,128)(2,1)S(1)} collective-permute-done((bf16[272,256]{1,0:T(8,128)(2,1)S(1)}, bf16[272,256]{1,0:T(8,128)(2,1)S(1)}, u32[]{:S(2)}, u32[]{:S(2)}) %collective-permute-start.4) | collective-permute-done | bytes 139296 | tf_op jit(solution)/shard_map/ppermute | solution.py:18
  21.0 0.0 collective-permute-done.3.refs_4_
  21.0 1.5 %collective-permute-done.1.refs_2_ = bf16[272,256]{1,0:T(8,128)(2,1)S(1)} collective-permute-done((bf16[272,256]{1,0:T(8,128)(2,1)S(1)}, bf16[272,256]{1,0:T(8,128)(2,1)S(1)}, u32[]{:S(2)}, u32[]{:S(2)}) %collective-permute-start.1) | collective-permute-done | bytes 139296 | tf_op jit(solution)/shard_map/ppermute | solution.py:18
  22.5 6.0 %collective-permute-done.refs_1_ = bf16[272,256]{1,0:T(8,128)(2,1)S(1)} collective-permute-done((bf16[272,256]{1,0:T(8,128)(2,1)S(1)}, bf16[272,256]{1,0:T(8,128)(2,1)S(1)}, u32[]{:S(2)}, u32[]{:S(2)}) %collective-permute-start) | collective-permute-done | bytes 139296 | tf_op jit(solution)/shard_map/ppermute | solution.py:18
  28.5 1.0 %copy-done = bf16[256,1024]{1,0:T(8,128)(2,1)S(1)} copy-done((bf16[256,1024]{1,0:T(8,128)(2,1)S(1)}, bf16[256,1024]{1,0:T(8,128)(2,1)}, u32[]{:S(2)}) %copy-start) | copy-done | bytes 524312
  29.5 1.0 %copy-done.1 = bf16[256,1024]{1,0:T(8,128)(2,1)S(1)} copy-done((bf16[256,1024]{1,0:T(8,128)(2,1)S(1)}, bf16[256,1024]{1,0:T(8,128)(2,1)}, u32[]{:S(2)}) %copy-start.1) | copy-done | bytes 524312
  30.5 32.3 %attention.1 = (bf16[256,1024]{1,0:T(8,128)(2,1)}, bf16[256,1024]{1,0:T(8,128)(2,1)}, f32[256,256]{1,0:T(8,128)S(1)}, bf16[256,256]{1,0:T(8,128)(2,1)S(1)}, bf16...) custom-call(bf16[256,1024]{1,0:T(8,128)(2,1)S(1)} %copy-done, ...), custom_call_target="tpu_custom_call" | custom-call | tf_op jit(solution)/shard_map/attention/pallas_call | solution.py:123
  62.9 0.4 collective-permute-start.8
  63.3 2.3 %collective-permute-start.10 = (bf16[256,256]{1,0:T(8,128)(2,1)S(1)}, bf16[256,256]{1,0:T(8,128)(2,1)S(1)}, u32[]{:S(2)}, u32[]{:S(2)}) collective-permute-start(bf16[256,256]{1,0:T(8,128)(2,1)S(1)} %get-tuple-element.20), channel_id=1, source_target_pairs={{0,251},{1,252},{2,253},{3,254},{4,255},{5,0},{6,1},{7,2},{8,3},{9... | collective-permute-start | bytes 393224 | tf_op jit(solution)/shard_map/ppermute | solution.py:18
  65.6 5.8 %collective-permute-done.6 = bf16[256,256]{1,0:T(8,128)(2,1)S(1)} collective-permute-done((bf16[256,256]{1,0:T(8,128)(2,1)S(1)}, bf16[256,256]{1,0:T(8,128)(2,1)S(1)}, u32[]{:S(2)}, u32[]{:S(2)}) %collective-permute-start.6) | collective-permute-done | bytes 131104 | tf_op jit(solution)/shard_map/ppermute | solution.py:18
  71.5 0.7 collective-permute-done.8
  72.1 0.2 collective-permute-done.9
  72.4 1.4 %collective-permute-done.10 = bf16[256,256]{1,0:T(8,128)(2,1)S(1)} collective-permute-done((bf16[256,256]{1,0:T(8,128)(2,1)S(1)}, bf16[256,256]{1,0:T(8,128)(2,1)S(1)}, u32[]{:S(2)}, u32[]{:S(2)}) %collective-permute-start.10) | collective-permute-done | bytes 131104 | tf_op jit(solution)/shard_map/ppermute | solution.py:18
  73.8 3.6 %collective-permute-done.11 = bf16[256,256]{1,0:T(8,128)(2,1)S(1)} collective-permute-done((bf16[256,256]{1,0:T(8,128)(2,1)S(1)}, bf16[256,256]{1,0:T(8,128)(2,1)S(1)}, u32[]{:S(2)}, u32[]{:S(2)}) %collective-permute-start.11) | collective-permute-done | bytes 131104 | tf_op jit(solution)/shard_map/ppermute | solution.py:18
  77.4 0.1 convert_add_fusion
  77.5 0.7 fusion
  (10 shorter events, 0.0 us)
Async XLA Ops:
  2.2 16.3 %collective-permute-start.5 = (bf16[272,256]{1,0:T(8,128)(2,1)S(1)}, bf16[272,256]{1,0:T(8,128)(2,1)S(1)}, u32[]{:S(2)}, u32[]{:S(2)}) collective-permute-start(bf16[272,256]{1,0:T(8,128)(2,1)S(1)} %pad_maximum_fusion.refs_0_), channel_id=1, source_target_pairs={{0,6},{1,7},{2,8},{3,9},{4,10},{5,11},{6,12},{7,13},{8,14},{9,15},... | collective-permute-start | bytes 417800 | tf_op jit(solution)/shard_map/ppermute | solution.py:18
  3.0 17.9 %collective-permute-start.4 = (bf16[272,256]{1,0:T(8,128)(2,1)S(1)}, bf16[272,256]{1,0:T(8,128)(2,1)S(1)}, u32[]{:S(2)}, u32[]{:S(2)}) collective-permute-start(bf16[272,256]{1,0:T(8,128)(2,1)S(1)} %pad_maximum_fusion.refs_0_), channel_id=1, source_target_pairs={{0,5},{1,6},{2,7},{3,8},{4,9},{5,10},{6,11},{7,12},{8,13},{9,14},{... | collective-permute-start | bytes 417800 | tf_op jit(solution)/shard_map/ppermute | solution.py:18
  4.9 16.1 %collective-permute-start.3 = (bf16[272,256]{1,0:T(8,128)(2,1)S(1)}, bf16[272,256]{1,0:T(8,128)(2,1)S(1)}, u32[]{:S(2)}, u32[]{:S(2)}) collective-permute-start(bf16[272,256]{1,0:T(8,128)(2,1)S(1)} %pad_maximum_fusion.refs_0_), channel_id=1, source_target_pairs={{0,4},{1,5},{2,6},{3,7},{4,8},{5,9},{6,10},{7,11},{8,12},{9,13},{1... | collective-permute-start | bytes 417800 | tf_op jit(solution)/shard_map/ppermute | solution.py:18
  4.9 16.1 %collective-permute-start.2 = (bf16[272,256]{1,0:T(8,128)(2,1)S(1)}, bf16[272,256]{1,0:T(8,128)(2,1)S(1)}, u32[]{:S(2)}, u32[]{:S(2)}) collective-permute-start(bf16[272,256]{1,0:T(8,128)(2,1)S(1)} %pad_maximum_fusion.refs_0_), channel_id=1, source_target_pairs={{0,3},{1,4},{2,5},{3,6},{4,7},{5,8},{6,9},{7,10},{8,11},{9,12},{10... | collective-permute-start | bytes 417800 | tf_op jit(solution)/shard_map/ppermute | solution.py:18
  8.7 13.8 %collective-permute-start.1 = (bf16[272,256]{1,0:T(8,128)(2,1)S(1)}, bf16[272,256]{1,0:T(8,128)(2,1)S(1)}, u32[]{:S(2)}, u32[]{:S(2)}) collective-permute-start(bf16[272,256]{1,0:T(8,128)(2,1)S(1)} %pad_maximum_fusion.refs_0_), channel_id=1, source_target_pairs={{0,2},{1,3},{2,4},{3,5},{4,6},{5,7},{6,8},{7,9},{8,10},{9,11},{10,... | collective-permute-start | bytes 417800 | tf_op jit(solution)/shard_map/ppermute | solution.py:18
  18.5 9.9 %collective-permute-start = (bf16[272,256]{1,0:T(8,128)(2,1)S(1)}, bf16[272,256]{1,0:T(8,128)(2,1)S(1)}, u32[]{:S(2)}, u32[]{:S(2)}) collective-permute-start(bf16[272,256]{1,0:T(8,128)(2,1)S(1)} %pad_maximum_fusion.refs_0_), channel_id=1, source_target_pairs={{0,1},{1,2},{2,3},{3,4},{4,5},{5,6},{6,7},{7,8},{8,9},{9,10},{10,1... | collective-permute-start | bytes 417800 | tf_op jit(solution)/shard_map/ppermute | solution.py:18
  28.5 1.0 %copy-start = (bf16[256,1024]{1,0:T(8,128)(2,1)S(1)}, bf16[256,1024]{1,0:T(8,128)(2,1)}, u32[]{:S(2)}) copy-start(bf16[256,1024]{1,0:T(8,128)(2,1)} %q_ref.1) | copy-start | bytes 1572868
  29.5 1.0 %copy-start.1 = (bf16[256,1024]{1,0:T(8,128)(2,1)S(1)}, bf16[256,1024]{1,0:T(8,128)(2,1)}, u32[]{:S(2)}) copy-start(bf16[256,1024]{1,0:T(8,128)(2,1)} %g_ref.1) | copy-start | bytes 1572868
  62.9 8.6 %collective-permute-start.6 = (bf16[256,256]{1,0:T(8,128)(2,1)S(1)}, bf16[256,256]{1,0:T(8,128)(2,1)S(1)}, u32[]{:S(2)}, u32[]{:S(2)}) collective-permute-start(bf16[256,256]{1,0:T(8,128)(2,1)S(1)} %get-tuple-element.16), channel_id=1, source_target_pairs={{0,255},{1,0},{2,1},{3,2},{4,3},{5,4},{6,5},{7,6},{8,7},{9,8},{10,... | collective-permute-start | bytes 393224 | tf_op jit(solution)/shard_map/ppermute | solution.py:18
  62.9 8.6 %collective-permute-start.7 = (bf16[256,256]{1,0:T(8,128)(2,1)S(1)}, bf16[256,256]{1,0:T(8,128)(2,1)S(1)}, u32[]{:S(2)}, u32[]{:S(2)}) collective-permute-start(bf16[256,256]{1,0:T(8,128)(2,1)S(1)} %get-tuple-element.17), channel_id=1, source_target_pairs={{0,254},{1,255},{2,0},{3,1},{4,2},{5,3},{6,4},{7,5},{8,6},{9,7},{1... | collective-permute-start | bytes 393224 | tf_op jit(solution)/shard_map/ppermute | solution.py:18
  62.9 9.3 %collective-permute-start.8 = (bf16[256,256]{1,0:T(8,128)(2,1)S(1)}, bf16[256,256]{1,0:T(8,128)(2,1)S(1)}, u32[]{:S(2)}, u32[]{:S(2)}) collective-permute-start(bf16[256,256]{1,0:T(8,128)(2,1)S(1)} %get-tuple-element.18), channel_id=1, source_target_pairs={{0,253},{1,254},{2,255},{3,0},{4,1},{5,2},{6,3},{7,4},{8,5},{9,6},... | collective-permute-start | bytes 393224 | tf_op jit(solution)/shard_map/ppermute | solution.py:18
  63.3 9.1 %collective-permute-start.9 = (bf16[256,256]{1,0:T(8,128)(2,1)S(1)}, bf16[256,256]{1,0:T(8,128)(2,1)S(1)}, u32[]{:S(2)}, u32[]{:S(2)}) collective-permute-start(bf16[256,256]{1,0:T(8,128)(2,1)S(1)} %get-tuple-element.19), channel_id=1, source_target_pairs={{0,252},{1,253},{2,254},{3,255},{4,0},{5,1},{6,2},{7,3},{8,4},{9,5... | collective-permute-start | bytes 393224 | tf_op jit(solution)/shard_map/ppermute | solution.py:18
  63.3 10.5 %collective-permute-start.10 = (bf16[256,256]{1,0:T(8,128)(2,1)S(1)}, bf16[256,256]{1,0:T(8,128)(2,1)S(1)}, u32[]{:S(2)}, u32[]{:S(2)}) collective-permute-start(bf16[256,256]{1,0:T(8,128)(2,1)S(1)} %get-tuple-element.20), channel_id=1, source_target_pairs={{0,251},{1,252},{2,253},{3,254},{4,255},{5,0},{6,1},{7,2},{8,3},{9... | collective-permute-start | bytes 393224 | tf_op jit(solution)/shard_map/ppermute | solution.py:18
  71.5 5.9 %collective-permute-start.11 = (bf16[256,256]{1,0:T(8,128)(2,1)S(1)}, bf16[256,256]{1,0:T(8,128)(2,1)S(1)}, u32[]{:S(2)}, u32[]{:S(2)}) collective-permute-start(bf16[256,256]{1,0:T(8,128)(2,1)S(1)} %get-tuple-element.21), channel_id=1, source_target_pairs={{0,250},{1,251},{2,252},{3,253},{4,254},{5,255},{6,0},{7,1},{8,2},... | collective-permute-start | bytes 393224 | tf_op jit(solution)/shard_map/ppermute | solution.py:18

commit v2 on v1

v2 whole, which is shorter than its diff:
```python
import functools
import math

import jax
import jax.numpy as jnp
from jax import lax
from jax.experimental import pallas as pl
from jax.experimental.pallas import tpu as pltpu
from jax.sharding import PartitionSpec as P

AXES = ("seq", "grp")
NEAR = 3
FAR = 3
NEAR_SIZES = (2, 4)
FAR_SIZES = (0, 1, 3)
GROUP = 2
HIDE = -1e30


def wrapped(value, steps):
    count = lax.axis_size(AXES)
    return lax.ppermute(value, AXES, [(i, (i + steps) % count) for i in range(count)])


def dot(a, b, over_a, over_b):
    return lax.dot_general(
        a, b, (((over_a,), (over_b,)), ((), ())), preferred_element_type=jnp.float32
    )


def nt(a, b):
    return dot(a, b, 1, 1)


def nn(a, b):
    return dot(a, b, 1, 0)


def tn(a, b):
    return dot(a, b, 0, 0)


def rows(c, size):
    return slice(c * size, (c + 1) * size)


def at(h, size):
    return pl.ds(pl.multiple_of(h * size, size), size)


def marks_of(block, tokens):
    return block[tokens : tokens + 8, :].astype(jnp.float32)


def reached(seg_row, first):
    return jnp.sum(jnp.where(seg_row == first, 1.0, 0.0), axis=1, keepdims=True)


def bias_of(seg_row, row_seg, first, key_at):
    tokens = key_at.shape[0]
    count = reached(seg_row, first)
    shown = (key_at.astype(jnp.float32) >= tokens - count) & (row_seg == first)
    return jnp.where(shown, 0.0, HIDE), jnp.where(count > 0, 1.0, 0.0)


def for_heads(heads, needed, sizes, step):
    below = -1
    for size in sizes:

        @pl.when((needed > below) & (needed <= size))
        def _(size=size):
            def group(i, carry):
                step([i * GROUP + k for k in range(GROUP)], size)
                return carry

            lax.fori_loop(0, heads // GROUP, group, 0)

        below = size


def fold(op, x):
    return op(x.reshape(-1, 8, x.shape[1]), axis=0)


def near_forward(heads, q_ref, *refs):
    blocks = refs[: NEAR + 1]
    e_ref, o_ref, stat_ref, ks, vs, bias, *sc = refs[NEAR + 1 :]
    tokens = q_ref.shape[0]
    width = q_ref.shape[1] // heads
    scale2 = width**-0.5 * math.log2(math.e)
    own_seg = marks_of(blocks[0], tokens)
    row_seg = own_seg[0:1, :]
    key_seg = jnp.transpose(own_seg)[:, 0:1]
    key_at = lax.broadcasted_iota(jnp.int32, (tokens, tokens), 0)
    row_at = lax.broadcasted_iota(jnp.int32, (tokens, tokens), 1)
    bias[rows(0, tokens), :] = jnp.where((key_seg == row_seg) & (key_at <= row_at), 0.0, HIDE)
    first = row_seg[:, 0:1]
    reach = jnp.ones((1, 1), jnp.float32)
    for c in range(1, NEAR + 1):
        bias[rows(c, tokens), :], more = bias_of(
            marks_of(blocks[c], tokens)[0:1, :], row_seg, first, key_at
        )
        reach = reach + more
    for c in range(NEAR + 1):
        ks[rows(c, tokens), :] = blocks[c][0:tokens, 0:width]
        vs[rows(c, tokens), :] = blocks[c][0:tokens, width : 2 * width]

    def step(hs, size):
        for k, h in enumerate(hs):
            q = q_ref[:, at(h, width)]
            top = jnp.full((8, tokens), HIDE, jnp.float32)
            for c in range(size):
                r = rows(c, tokens)
                s = nt(ks[r, :], q) * scale2 + bias[r, :]
                sc[k][r, :] = s
                top = jnp.maximum(top, fold(jnp.max, s))
            top = jnp.max(top, axis=0, keepdims=True)
            total = jnp.zeros((8, tokens), jnp.float32)
            for c in range(size):
                r = rows(c, tokens)
                e = jnp.exp2(sc[k][r, :] - top)
                total = total + fold(jnp.sum, e)
                e_ref[r, at(h, tokens)] = e.astype(jnp.bfloat16)
            total = jnp.sum(total, axis=0, keepdims=True)
            stat_ref[0:8, at(h, tokens)] = jnp.broadcast_to(top, (8, tokens))
            stat_ref[8:16, at(h, tokens)] = jnp.broadcast_to(total, (8, tokens))
        seen = slice(0, size * tokens)
        for h in hs:
            o_ref[:, at(h, width)] = tn(e_ref[seen, at(h, tokens)], vs[seen, :])

    for_heads(heads, jnp.sum(reach).astype(jnp.int32), NEAR_SIZES, step)


def far_both(heads, q_ref, g_ref, near_out, stat_ref, own, far, *refs):
    o_ref, part, dq_ref, gn_ref, dots_ref, ks, vs, bias, sums, *slots = refs
    sc, ex, ds, gf, dt = (slots[i * GROUP : (i + 1) * GROUP] for i in range(5))
    tokens = q_ref.shape[0]
    width = q_ref.shape[1] // heads
    scale = width**-0.5
    scale2 = scale * math.log2(math.e)
    pitch = far.shape[0] // FAR
    row_seg = marks_of(own, tokens)[0:1, :]
    first = row_seg[:, 0:1]
    key_at = lax.broadcasted_iota(jnp.int32, (tokens, tokens), 0)
    reach = jnp.zeros((1, 1), jnp.float32)
    for c in range(FAR):
        seg = far[c * pitch + tokens : c * pitch + tokens + 8, :].astype(jnp.float32)[0:1, :]
        bias[rows(c, tokens), :], more = bias_of(seg, row_seg, first, key_at)
        reach = reach + more
        ks[rows(c, tokens), :] = far[c * pitch : c * pitch + tokens, 0:width]
        vs[rows(c, tokens), :] = far[c * pitch : c * pitch + tokens, width : 2 * width]
    sums[...] = jnp.zeros_like(sums)

    def step(hs, size):
        seen = slice(0, size * tokens)
        for k, h in enumerate(hs):
            q = q_ref[:, at(h, width)]
            lanes = at(h, tokens)
            old = stat_ref[0:1, lanes]
            top = jnp.broadcast_to(old, (8, tokens))
            for c in range(size):
                r = rows(c, tokens)
                s = nt(ks[r, :], q) * scale2 + bias[r, :]
                sc[k][r, :] = s
                top = jnp.maximum(top, fold(jnp.max, s))
            top = jnp.max(top, axis=0, keepdims=True)
            keep = jnp.exp2(old - top)
            total = jnp.zeros((8, tokens), jnp.float32)
            for c in range(size):
                r = rows(c, tokens)
                e = jnp.exp2(sc[k][r, :] - top)
                total = total + fold(jnp.sum, e)
                ex[k][r, :] = e.astype(jnp.bfloat16)
            total = jnp.sum(total, axis=0, keepdims=True) + stat_ref[8:9, lanes] * keep
            inv = 1.0 / total
            near = inv * keep
            both = jnp.concatenate(
                [jnp.broadcast_to(inv, (8, tokens)), jnp.broadcast_to(near, (8, tokens))], axis=0
            )
            cols = jnp.transpose(both)
            inv_rows, near_rows = cols[:, 0:1], cols[:, 8:9]
            g = g_ref[:, at(h, width)].astype(jnp.float32)
            gf[k][...] = (g * inv_rows).astype(jnp.bfloat16)
            gn_ref[lanes, :] = (g * near_rows).astype(jnp.bfloat16)
            out = near_out[:, at(h, width)] * near_rows
            if size:
                out = out + tn(ex[k][seen, :], vs[seen, :]) * inv_rows
            o_ref[:, at(h, width)] = out.astype(o_ref.dtype)
            prod = g * out
            high = prod.astype(jnp.bfloat16)
            low = (prod - high.astype(jnp.float32)).astype(jnp.bfloat16)
            ones = jnp.ones((8, width), jnp.bfloat16)
            dots = nt(ones, high) + nt(ones, low)
            dots_ref[:, lanes] = dots * near
            dt[k][...] = dots * inv
        for k, h in enumerate(hs):
            lanes = at(h, width)
            if not size:
                dq_ref[:, lanes] = jnp.zeros((tokens, width), jnp.float32)
                continue
            q = q_ref[:, lanes]
            g = gf[k][...]
            sums[seen, width : 2 * width] += nn(ex[k][seen, :], g)
            for c in range(size):
                r = rows(c, tokens)
                d = nt(vs[r, :], g) - dt[k][0:1, :]
                ds[k][r, :] = (ex[k][r, :].astype(jnp.float32) * d).astype(jnp.bfloat16)
            sums[seen, 0:width] += nn(ds[k][seen, :], q)
            dq_ref[:, lanes] = tn(ds[k][seen, :], ks[seen, :])

    for_heads(heads, jnp.sum(reach).astype(jnp.int32), FAR_SIZES, step)
    part[:, 0:width] = (sums[:, 0:width] * scale).astype(part.dtype)
    part[:, width : 2 * width] = sums[:, width : 2 * width].astype(part.dtype)


def near_backward(heads, q_ref, gn_ref, dots_ref, e_ref, far_dq, *refs):
    blocks = refs[: NEAR + 1]
    dq_ref, sums, ks, vs, *ds = refs[NEAR + 1 :]
    tokens = q_ref.shape[0]
    width = q_ref.shape[1] // heads
    scale = width**-0.5
    row_seg = marks_of(blocks[0], tokens)[0:1, :]
    reach = jnp.ones((1, 1), jnp.float32)
    for c in range(1, NEAR + 1):
        count = reached(marks_of(blocks[c], tokens)[0:1, :], row_seg[:, 0:1])
        reach = reach + jnp.where(count > 0, 1.0, 0.0)
    for c in range(NEAR + 1):
        ks[rows(c, tokens), :] = blocks[c][0:tokens, 0:width]
        vs[rows(c, tokens), :] = blocks[c][0:tokens, width : 2 * width]
    sums[...] = jnp.zeros_like(sums)

    def step(hs, size):
        seen = slice(0, size * tokens)
        for k, h in enumerate(hs):
            g = gn_ref[at(h, tokens), :]
            lanes = at(h, tokens)
            sums[seen, width : 2 * width] += nn(e_ref[seen, lanes], g)
            for c in range(size):
                r = rows(c, tokens)
                d = nt(vs[r, :], g) - dots_ref[0:1, lanes]
                ds[k][r, :] = (e_ref[r, lanes].astype(jnp.float32) * d).astype(jnp.bfloat16)
        for k, h in enumerate(hs):
            lanes = at(h, width)
            sums[seen, 0:width] += nn(ds[k][seen, :], q_ref[:, lanes])
            dq = far_dq[:, lanes] + tn(ds[k][seen, :], ks[seen, :])
            dq_ref[:, lanes] = (dq * scale).astype(dq_ref.dtype)

    for_heads(heads, jnp.sum(reach).astype(jnp.int32), NEAR_SIZES, step)
    sums[:, 0:width] = sums[:, 0:width] * scale


def add_parts(sums, far, *outs):
    tokens = outs[0].shape[0]
    for d, out in enumerate(outs):
        total = sums[rows(d + 1, tokens), :] + far[rows(d, tokens), :].astype(jnp.float32)
        out[...] = total.astype(out.dtype)


VM = pl.BlockSpec(memory_space=pltpu.VMEM)


def call(kernel, name, args, outs, scratch, flops):
    return pl.pallas_call(
        kernel,
        out_shape=tuple(jax.ShapeDtypeStruct(*o) for o in outs),
        in_specs=[VM] * len(args),
        out_specs=(VM,) * len(outs),
        scratch_shapes=[pltpu.VMEM(*s) for s in scratch],
        compiler_params=pltpu.CompilerParams(vmem_limit_bytes=24 * 1024 * 1024),
        cost_estimate=pl.CostEstimate(flops=flops, bytes_accessed=1 << 21, transcendentals=0),
        name=name,
    )(*args)


BF, F32 = jnp.bfloat16, jnp.float32


def dims(queries, own):
    tokens = queries.shape[0]
    width = own.shape[1] // 2
    return tokens, width, queries.shape[1] // width


def run_near_forward(queries, near):
    tokens, width, heads = dims(queries, near[0])
    keys, all_rows = (NEAR + 1) * tokens, heads * tokens
    return call(
        functools.partial(near_forward, heads),
        "near_forward",
        (queries, *near),
        [((keys, all_rows), BF), (queries.shape, F32), ((16, all_rows), F32)],
        [((keys, width), BF)] * 2 + [((keys, tokens), F32)] * (1 + GROUP),
        4 * keys * all_rows * width,
    )


def run_far(queries, out_grad, near_out, stats, own, far):
    tokens, width, heads = dims(queries, own)
    keys, all_rows = FAR * tokens, heads * tokens
    return call(
        functools.partial(far_both, heads),
        "far_both",
        (queries, out_grad, near_out, stats, own, far),
        [
            (queries.shape, BF),
            ((keys, 2 * width), BF),
            (queries.shape, F32),
            ((all_rows, width), BF),
            ((8, all_rows), F32),
        ],
        [((keys, width), BF)] * 2
        + [((keys, tokens), F32), ((keys, 2 * width), F32)]
        + [((keys, tokens), F32)] * GROUP
        + [((keys, tokens), BF)] * (2 * GROUP)
        + [((tokens, width), BF)] * GROUP
        + [((8, tokens), F32)] * GROUP,
        10 * keys * all_rows * width,
    )


def run_near_backward(queries, near_grad, dots, weights, far_dq, near):
    tokens, width, heads = dims(queries, near[0])
    keys, all_rows = (NEAR + 1) * tokens, heads * tokens
    return call(
        functools.partial(near_backward, heads),
        "near_backward",
        (queries, near_grad, dots, weights, far_dq, *near),
        [(queries.shape, BF), ((keys, 2 * width), F32)],
        [((keys, width), BF)] * 2 + [((keys, tokens), BF)] * GROUP,
        8 * keys * all_rows * width,
    )


def run_add(sums, far):
    tokens = far.shape[0] // FAR
    return call(add_parts, "add_parts", (sums, far), [((tokens, far.shape[1]), BF)] * NEAR, [], 1)


def on_device(queries, key_rows, value_rows, out_grad, segment):
    tokens, width = key_rows.shape
    marks = jnp.broadcast_to(segment.astype(jnp.bfloat16)[None, :], (16, tokens))
    own = jnp.concatenate([jnp.concatenate([key_rows, value_rows], axis=1), marks], axis=0)
    near = [own] + [wrapped(own, d) for d in range(1, NEAR + 1)]
    far = wrapped(jnp.concatenate(near[1:], axis=0), NEAR)
    weights, near_out, stats = run_near_forward(queries, near)
    attended, far_part, far_dq, near_grad, dots = run_far(
        queries, out_grad, near_out, stats, own, far
    )
    far_back = wrapped(far_part, -NEAR)
    query_grad, sums = run_near_backward(queries, near_grad, dots, weights, far_dq, near)
    total = sums[:tokens]
    for d, part in enumerate(run_add(sums, far_back)):
        total = total + wrapped(part, -d - 1).astype(jnp.float32)
    return attended, query_grad, total[:, :width], total[:, width:]


def solution(mesh):
    spec = P(AXES, None)
    return jax.shard_map(
        on_device,
        mesh=mesh,
        in_specs=(spec, spec, spec, spec, P(AXES)),
        out_specs=(spec,) * 4,
        check_vma=False,
    )
```

time: 79.5 us -> 64 us (0.81); the launches traced: 78.2 us -> 65.1 us
  Pallas kernels: 32.3 us -> 10.9 us
  starting transfers between devices: 9.28 us -> 21 us
  waiting for transfers between devices: 31.4 us -> 29.1 us
  local copies, waits for them, and re-layouts: 2.81 us -> 1.76 us
    pallas_call x1 -> x4, Pallas kernels: 32.3 us -> 10.9 us  [call(): pl.pallas_call(kernel, out_shape=tuple((jax.ShapeDtypeStruct(*o) for o in...]
    ppermute x12 -> x8, starting transfers between devices: 9.28 us -> 21 us  [wrapped(): lax.ppermute(value, AXES, [(i, (i + steps) % count) for i in range(count)])]
    ppermute x12 -> x8, waiting for transfers between devices: 31.4 us -> 29.1 us  [wrapped(): lax.ppermute(value, AXES, [(i, (i + steps) % count) for i in range(count)])]
    unnamed x4, local copies, waits for them, and re-layouts: 2.08 us -> 1.04 us
  transfers between devices with their start and end apart: 12 -> 8, of which waited for: 9 -> 8; matrix products, arithmetic and copies ran while one was open for 0% -> 0% of each run, Pallas kernels for 0% -> 12%
where the time goes in v2:
time: 64 us; the launch traced here: 65.1 us
  waiting for transfers between devices  29.1 us (45%)
  starting transfers between devices  21 us (33%)
  Pallas kernels  10.9 us (17%)
  local copies, waits for them, and re-layouts  1.76 us (3%)
  other arithmetic  1.71 us (3%)
  between operations  0.69 us (1%)
    ppermute x8, waiting for transfers between devices, wrapped(): lax.ppermute(value, AXES, [(i, (i + steps) % count) for i in range(count)])  29.1 us
    ppermute x8, starting transfers between devices, wrapped(): lax.ppermute(value, AXES, [(i, (i + steps) % count) for i in range(count)])  21 us
    pallas_call x4, Pallas kernels, call(): pl.pallas_call(kernel, out_shape=tuple((jax.ShapeDtypeStruct(*o) for o in...  10.9 us
  transfers between devices with their start and end apart: 8, of which 8 were waited for; matrix products, arithmetic and copies ran while one was open for 0% of the time, Pallas kernels for 12%

profile of v2, /device:TPU:0, one launch (start us, length us, event | category | flops | bytes accessed | tf_op | source)
XLA Modules:
  0.0 65.1 jit_solution(8916417545181772430)
XLA Ops:
  0.6 0.7 %convert_element_type.12 = bf16[256]{0:T(256)(128)(2,1)S(1)} convert(s32[256]{0:T(256)} %param.9) | non-fusion elementwise | flops 256 | bytes 1536 | tf_op jit(solution)/shard_map/convert_element_type | solution.py:341
  1.4 0.9 %pad_maximum_fusion.1.refs_0_.own = bf16[272,256]{1,0:T(8,128)(2,1)S(1)} fusion(bf16[16,256]{1,0:T(8,128)(2,1)S(1)} %broadcast_in_dim.2, bf16[256,128]{1,0:T(8,128)(2,1)} %param.7, bf16[256,128]{1,0:T(8,128)(2,1)} %param.6), kind=kLoop, calls=%fused_computation.2 | loop fusion | flops 417792 | bytes 278528 | tf_op jit(solution)/shard_map/concatenate | solution.py:342
  2.3 1.1 %collective-permute-start.2 = (bf16[272,256]{1,0:T(8,128)(2,1)S(1)}, bf16[272,256]{1,0:T(8,128)(2,1)S(1)}, u32[]{:S(2)}, u32[]{:S(2)}) collective-permute-start(bf16[272,256]{1,0:T(8,128)(2,1)S(1)} %pad_maximum_fusion.1.refs_0_.own), channel_id=1, source_target_pairs={{0,3},{1,4},{2,5},{3,6},{4,7},{5,8},{6,9},{7,10},{8,11},{9,12},{10... | collective-permute-start | bytes 417800 | tf_op jit(solution)/shard_map/ppermute | solution.py:22
  3.4 0.4 collective-permute-start.1
  3.8 0.8 %collective-permute-start = (bf16[272,256]{1,0:T(8,128)(2,1)S(1)}, bf16[272,256]{1,0:T(8,128)(2,1)S(1)}, u32[]{:S(2)}, u32[]{:S(2)}) collective-permute-start(bf16[272,256]{1,0:T(8,128)(2,1)S(1)} %pad_maximum_fusion.1.refs_0_.own), channel_id=1, source_target_pairs={{0,1},{1,2},{2,3},{3,4},{4,5},{5,6},{6,7},{7,8},{8,9},{9,10},{10,1... | collective-permute-start | bytes 417800 | tf_op jit(solution)/shard_map/ppermute | solution.py:22
  4.5 7.6 %collective-permute-done.2.refs_3_ = bf16[272,256]{1,0:T(8,128)(2,1)S(1)} collective-permute-done((bf16[272,256]{1,0:T(8,128)(2,1)S(1)}, bf16[272,256]{1,0:T(8,128)(2,1)S(1)}, u32[]{:S(2)}, u32[]{:S(2)}) %collective-permute-start.2) | collective-permute-done | bytes 139296 | tf_op jit(solution)/shard_map/ppermute | solution.py:22
  12.1 3.3 %collective-permute-done.1.refs_2_ = bf16[272,256]{1,0:T(8,128)(2,1)S(1)} collective-permute-done((bf16[272,256]{1,0:T(8,128)(2,1)S(1)}, bf16[272,256]{1,0:T(8,128)(2,1)S(1)}, u32[]{:S(2)}, u32[]{:S(2)}) %collective-permute-start.1) | collective-permute-done | bytes 139296 | tf_op jit(solution)/shard_map/ppermute | solution.py:22
  15.5 1.2 %collective-permute-done.refs_1_ = bf16[272,256]{1,0:T(8,128)(2,1)S(1)} collective-permute-done((bf16[272,256]{1,0:T(8,128)(2,1)S(1)}, bf16[272,256]{1,0:T(8,128)(2,1)S(1)}, u32[]{:S(2)}, u32[]{:S(2)}) %collective-permute-start) | collective-permute-done | bytes 139296 | tf_op jit(solution)/shard_map/ppermute | solution.py:22
  16.7 0.1 collective-permute-start.3
  16.8 0.0 copy-start.1
  16.8 1.0 %copy-done.1 = bf16[256,1024]{1,0:T(8,128)(2,1)S(1)} copy-done((bf16[256,1024]{1,0:T(8,128)(2,1)S(1)}, bf16[256,1024]{1,0:T(8,128)(2,1)}, u32[]{:S(2)}) %copy-start.1) | copy-done | bytes 524312
  17.8 3.7 %near_forward.1 = (bf16[1024,2048]{1,0:T(8,128)(2,1)S(1)}, f32[256,1024]{1,0:T(8,128)S(1)}, f32[16,2048]{1,0:T(8,128)S(1)}) custom-call(bf16[256,1024]{1,0:T(8,128)(2,1)S(1)} %copy-done.1, bf16[272,256]{1,0:T(8,128)(2,1)S(1)} %pad_maximum_fusion.1.refs_0_.own, bf16[272,256]{1,0:T(8,128)(2,1)S(1)} %collective-permute-done.refs_1_, ...), custom_call_target="tpu_custom_call" | custom-call | flops 1073741824 | bytes 2097152 | tf_op jit(solution)/shard_map/near_forward/pallas_call | solution.py:263
  21.5 6.9 %collective-permute-done.3.far = bf16[816,256]{1,0:T(8,128)(2,1)S(1)} collective-permute-done((bf16[816,256]{1,0:T(8,128)(2,1)S(1)}, bf16[816,256]{1,0:T(8,128)(2,1)S(1)}, u32[]{:S(2)}, u32[]{:S(2)}) %collective-permute-start.3) | collective-permute-done | bytes 417824 | tf_op jit(solution)/shard_map/ppermute | solution.py:22
  28.5 3.0 %far_both.1 = (bf16[256,1024]{1,0:T(8,128)(2,1)}, bf16[768,256]{1,0:T(8,128)(2,1)S(1)}, f32[256,1024]{1,0:T(8,128)S(1)}, bf16[2048,128]{1,0:T(8,128)(2,1)S(1)}, f32[8,2048]{1,0:T(8,128)S(1)}) custom-call(bf16[256,1024]{1,0:T(8,128)(2,1)S(1)} %copy-done.1, bf16[256,1024]{1,0:T(8,128)(2,1)S(1)} %copy-done, f32[256,1024]{1,0:T(8,128)S(1)} %get-tuple-element.17.near_out, ...), custom_call_target="tpu_custom_call" | custom-call | flops 2013265920 | bytes 2097152 | tf_op jit(solution)/shard_map/far_both/pallas_call | solution.py:263
  31.5 3.4 %collective-permute-start.4 = (bf16[768,256]{1,0:T(8,128)(2,1)S(1)}, bf16[768,256]{1,0:T(8,128)(2,1)S(1)}, u32[]{:S(2)}, u32[]{:S(2)}) collective-permute-start(bf16[768,256]{1,0:T(8,128)(2,1)S(1)} %get-tuple-element.26), channel_id=1, source_target_pairs={{0,253},{1,254},{2,255},{3,0},{4,1},{5,2},{6,3},{7,4},{8,5},{9,6},... | collective-permute-start | bytes 1179656 | tf_op jit(solution)/shard_map/ppermute | solution.py:22
  34.9 4.1 %near_backward.1 = (bf16[256,1024]{1,0:T(8,128)(2,1)}, f32[1024,256]{1,0:T(8,128)S(1)}) custom-call(bf16[256,1024]{1,0:T(8,128)(2,1)S(1)} %copy-done.1, bf16[2048,128]{1,0:T(8,128)(2,1)S(1)} %get-tuple-element.20.gn_ref, f32[8,2048]{1,0:T(8,128)S(1)} %get-tuple-element.21.dots_ref, bf16[1024,2048]{1,0:T(8,128)(2,1)S(1)} %get-tuple-element.22.e_ref, ...), custom_call_target="tpu_custom_call" | custom-call | flops 2147483648 | bytes 2097152 | tf_op jit(solution)/shard_map/near_backward/pallas_call | solution.py:263
  39.0 2.5 %collective-permute-done.4.far = bf16[768,256]{1,0:T(8,128)(2,1)S(1)} collective-permute-done((bf16[768,256]{1,0:T(8,128)(2,1)S(1)}, bf16[768,256]{1,0:T(8,128)(2,1)S(1)}, u32[]{:S(2)}, u32[]{:S(2)}) %collective-permute-start.4) | collective-permute-done | bytes 393248 | tf_op jit(solution)/shard_map/ppermute | solution.py:22
  41.4 0.1 add_parts.1
  41.5 15.3 %collective-permute-start.5 = (bf16[256,256]{1,0:T(8,128)(2,1)S(1)}, bf16[256,256]{1,0:T(8,128)(2,1)S(1)}, u32[]{:S(2)}, u32[]{:S(2)}) collective-permute-start(bf16[256,256]{1,0:T(8,128)(2,1)S(1)} %get-tuple-element.27), channel_id=1, source_target_pairs={{0,255},{1,0},{2,1},{3,2},{4,3},{5,4},{6,5},{7,6},{8,7},{9,8},{10,... | collective-permute-start | bytes 393224 | tf_op jit(solution)/shard_map/ppermute | solution.py:22
  56.8 2.5 %collective-permute-done.5 = bf16[256,256]{1,0:T(8,128)(2,1)S(1)} collective-permute-done((bf16[256,256]{1,0:T(8,128)(2,1)S(1)}, bf16[256,256]{1,0:T(8,128)(2,1)S(1)}, u32[]{:S(2)}, u32[]{:S(2)}) %collective-permute-start.5) | collective-permute-done | bytes 131104 | tf_op jit(solution)/shard_map/ppermute | solution.py:22
  59.3 4.1 %collective-permute-done.6 = bf16[256,256]{1,0:T(8,128)(2,1)S(1)} collective-permute-done((bf16[256,256]{1,0:T(8,128)(2,1)S(1)}, bf16[256,256]{1,0:T(8,128)(2,1)S(1)}, u32[]{:S(2)}, u32[]{:S(2)}) %collective-permute-start.6) | collective-permute-done | bytes 131104 | tf_op jit(solution)/shard_map/ppermute | solution.py:22
  63.4 1.0 %collective-permute-done.7 = bf16[256,256]{1,0:T(8,128)(2,1)S(1)} collective-permute-done((bf16[256,256]{1,0:T(8,128)(2,1)S(1)}, bf16[256,256]{1,0:T(8,128)(2,1)S(1)}, u32[]{:S(2)}, u32[]{:S(2)}) %collective-permute-start.7) | collective-permute-done | bytes 131104 | tf_op jit(solution)/shard_map/ppermute | solution.py:22
  64.4 0.1 convert_add_fusion
  64.4 0.7 %fusion = (f32[256,128]{1,0:T(8,128)}, f32[256,128]{1,0:T(8,128)}) fusion(f32[256,256]{1,0:T(8,128)S(1)} %convert_add_fusion), kind=kLoop, calls=%fused_computation.3 | loop fusion | bytes 524288 | tf_op jit(solution)/shard_map/slice | solution.py:354
  (6 shorter events, 0.0 us)
Async XLA Ops:
  0.6 27.8 %copy-start = (bf16[256,1024]{1,0:T(8,128)(2,1)S(1)}, bf16[256,1024]{1,0:T(8,128)(2,1)}, u32[]{:S(2)}) copy-start(bf16[256,1024]{1,0:T(8,128)(2,1)} %g_ref.1) | copy-start | bytes 1572868
  2.3 9.9 %collective-permute-start.2 = (bf16[272,256]{1,0:T(8,128)(2,1)S(1)}, bf16[272,256]{1,0:T(8,128)(2,1)S(1)}, u32[]{:S(2)}, u32[]{:S(2)}) collective-permute-start(bf16[272,256]{1,0:T(8,128)(2,1)S(1)} %pad_maximum_fusion.1.refs_0_.own), channel_id=1, source_target_pairs={{0,3},{1,4},{2,5},{3,6},{4,7},{5,8},{6,9},{7,10},{8,11},{9,12},{10... | collective-permute-start | bytes 417800 | tf_op jit(solution)/shard_map/ppermute | solution.py:22
  3.4 12.1 %collective-permute-start.1 = (bf16[272,256]{1,0:T(8,128)(2,1)S(1)}, bf16[272,256]{1,0:T(8,128)(2,1)S(1)}, u32[]{:S(2)}, u32[]{:S(2)}) collective-permute-start(bf16[272,256]{1,0:T(8,128)(2,1)S(1)} %pad_maximum_fusion.1.refs_0_.own), channel_id=1, source_target_pairs={{0,2},{1,3},{2,4},{3,5},{4,6},{5,7},{6,8},{7,9},{8,10},{9,11},{10,... | collective-permute-start | bytes 417800 | tf_op jit(solution)/shard_map/ppermute | solution.py:22
  3.8 12.9 %collective-permute-start = (bf16[272,256]{1,0:T(8,128)(2,1)S(1)}, bf16[272,256]{1,0:T(8,128)(2,1)S(1)}, u32[]{:S(2)}, u32[]{:S(2)}) collective-permute-start(bf16[272,256]{1,0:T(8,128)(2,1)S(1)} %pad_maximum_fusion.1.refs_0_.own), channel_id=1, source_target_pairs={{0,1},{1,2},{2,3},{3,4},{4,5},{5,6},{6,7},{7,8},{8,9},{9,10},{10,1... | collective-permute-start | bytes 417800 | tf_op jit(solution)/shard_map/ppermute | solution.py:22
  16.7 11.8 %collective-permute-start.3 = (bf16[816,256]{1,0:T(8,128)(2,1)S(1)}, bf16[816,256]{1,0:T(8,128)(2,1)S(1)}, u32[]{:S(2)}, u32[]{:S(2)}) collective-permute-start(bf16[816,256]{1,0:T(8,128)(2,1)S(1)} %pad_maximum_fusion), channel_id=1, source_target_pairs={{0,3},{1,4},{2,5},{3,6},{4,7},{5,8},{6,9},{7,10},{8,11},{9,12},{10... | collective-permute-start | bytes 1253384 | tf_op jit(solution)/shard_map/ppermute | solution.py:22
  16.8 1.0 %copy-start.1 = (bf16[256,1024]{1,0:T(8,128)(2,1)S(1)}, bf16[256,1024]{1,0:T(8,128)(2,1)}, u32[]{:S(2)}) copy-start(bf16[256,1024]{1,0:T(8,128)(2,1)} %q_ref.5) | copy-start | bytes 1572868
  31.5 10.0 %collective-permute-start.4 = (bf16[768,256]{1,0:T(8,128)(2,1)S(1)}, bf16[768,256]{1,0:T(8,128)(2,1)S(1)}, u32[]{:S(2)}, u32[]{:S(2)}) collective-permute-start(bf16[768,256]{1,0:T(8,128)(2,1)S(1)} %get-tuple-element.26), channel_id=1, source_target_pairs={{0,253},{1,254},{2,255},{3,0},{4,1},{5,2},{6,3},{7,4},{8,5},{9,6},... | collective-permute-start | bytes 1179656 | tf_op jit(solution)/shard_map/ppermute | solution.py:22
  41.5 17.8 %collective-permute-start.5 = (bf16[256,256]{1,0:T(8,128)(2,1)S(1)}, bf16[256,256]{1,0:T(8,128)(2,1)S(1)}, u32[]{:S(2)}, u32[]{:S(2)}) collective-permute-start(bf16[256,256]{1,0:T(8,128)(2,1)S(1)} %get-tuple-element.27), channel_id=1, source_target_pairs={{0,255},{1,0},{2,1},{3,2},{4,3},{5,4},{6,5},{7,6},{8,7},{9,8},{10,... | collective-permute-start | bytes 393224 | tf_op jit(solution)/shard_map/ppermute | solution.py:22
  56.8 6.6 %collective-permute-start.6 = (bf16[256,256]{1,0:T(8,128)(2,1)S(1)}, bf16[256,256]{1,0:T(8,128)(2,1)S(1)}, u32[]{:S(2)}, u32[]{:S(2)}) collective-permute-start(bf16[256,256]{1,0:T(8,128)(2,1)S(1)} %get-tuple-element.28), channel_id=1, source_target_pairs={{0,254},{1,255},{2,0},{3,1},{4,2},{5,3},{6,4},{7,5},{8,6},{9,7},{1... | collective-permute-start | bytes 393224 | tf_op jit(solution)/shard_map/ppermute | solution.py:22
  56.8 7.6 %collective-permute-start.7 = (bf16[256,256]{1,0:T(8,128)(2,1)S(1)}, bf16[256,256]{1,0:T(8,128)(2,1)S(1)}, u32[]{:S(2)}, u32[]{:S(2)}) collective-permute-start(bf16[256,256]{1,0:T(8,128)(2,1)S(1)} %get-tuple-element.29), channel_id=1, source_target_pairs={{0,253},{1,254},{2,255},{3,0},{4,1},{5,2},{6,3},{7,4},{8,5},{9,6},... | collective-permute-start | bytes 393224 | tf_op jit(solution)/shard_map/ppermute | solution.py:22
